TPU v7x, 32 devices: a whole 2x2x4 slice. The times are simulated.
32 devices in a mesh: shard: 8 (over z, y), tensor: 4 (over x, core).
Axes of the slice: x: 2, y: 2, z: 4, core: 2. Of those that a mesh axis runs over, the one named last changes fastest.
Arguments:
- gradient: bfloat16 [8, 1024, 1024], P(None, 'shard', 'tensor'), may hold values from -64 to 64, as said below
- momentum: float32 [8, 1024, 1024], P(None, 'shard', 'tensor'), may hold values from -64 to 64, as said below
Outputs:
- momentum_out: float32 [8, 1024, 1024], P(None, 'shard', 'tensor')
- update: float32 [8, 1024, 1024], P(None, 'shard', 'tensor')
Inputs may be any that keep to these rules, and one draw needn't show every extreme that they name: `gradient`: finite real values. `momentum`: finite real values.
All inputs are finite; a program needn't handle non-finite values.
Results may differ from a plain program's by a relative error of at most 0.0003.
Values sent between devices are 32-bit elements; how exact they have to be, the bound alone decides.
A program may use at most 64 MiB of HBM per device.

v0:
```python
import math

import jax
import jax.numpy as jnp
from jax import lax
from jax.sharding import PartitionSpec as P

D = 1024
BLOCK = 1024
ITERS = 3


first_coef = 3.4445
second_coef = -4.775
third_coef = 2.0315
decay_rate = 0.95


def product(left, right):
    return jnp.einsum(
        "ij,jl->il",
        left,
        right,
        precision=lax.Precision.HIGHEST,
        preferred_element_type=jnp.float32,
    )


def against(left, right):
    return jnp.einsum(
        "ij,lj->il",
        left,
        right,
        precision=lax.Precision.HIGHEST,
        preferred_element_type=jnp.float32,
    )


def per_device(gradient, momentum):
    widened = gradient.astype(jnp.float32)
    momentum_out = decay_rate * momentum + widened
    direction = widened + decay_rate * momentum_out
    by_owner = lax.all_to_all(direction, "shard", split_axis=0, concat_axis=0, tiled=True)
    row_pieces = lax.all_to_all(by_owner, "tensor", split_axis=1, concat_axis=2, tiled=True)
    piece_count = row_pieces.shape[0]
    piece_rows = row_pieces.shape[1]
    width = row_pieces.shape[2]
    iterate = row_pieces.reshape(piece_count * piece_rows, width)
    norm_total = lax.psum(jnp.sum(iterate * iterate), "tensor")
    iterate = iterate / (jnp.sqrt(norm_total) + 1e-07)
    for sweep_index in range(ITERS):
        full_rows = lax.all_gather(iterate, "tensor", axis=0, tiled=True)
        gram_rows = against(iterate, full_rows)
        full_gram = lax.all_gather(gram_rows, "tensor", axis=0, tiled=True)
        square_rows = product(gram_rows, full_gram)
        polynomial = second_coef * gram_rows + third_coef * square_rows
        iterate = first_coef * iterate + product(polynomial, full_rows)
    result = (0.2 * math.sqrt(max(BLOCK, D)) * iterate).reshape(piece_count, piece_rows, width)
    update = lax.all_to_all(
        lax.all_to_all(result, "shard", split_axis=0, concat_axis=0, tiled=True),
        "tensor",
        split_axis=2,
        concat_axis=1,
        tiled=True,
    )
    return (momentum_out, update)


def solution(mesh):
    placed = (P(None, "shard", "tensor"), P(None, "shard", "tensor"))
    return jax.shard_map(
        per_device,
        mesh=mesh,
        in_specs=placed,
        out_specs=(P(None, "shard", "tensor"), P(None, "shard", "tensor")),
        check_vma=False,
    )
```

profile of v0, /device:TPU:9, one launch (start us, length us, event | category | flops | bytes accessed | tf_op | source)
XLA Modules:
  0.0 403.0 jit_solution(4511318849442927990)
XLA Ops:
  7.2 2.5 convert_add_fusion
  9.8 29.4 %all_to_all.37 = f32[8,128,256]{2,1,0:T(8,128)S(1)} all-to-all(f32[8,128,256]{2,1,0:T(8,128)S(1)} %get-tuple-element.4), channel_id=1, replica_groups=mesh['shard'=8,'tensor'=4] {'shard'}, dimensions={0} | all-to-all | bytes 2097152 | tf_op jit(solution)/shard_map/all_to_all | solution.py:43
  39.2 0.6 copy.12
  39.8 18.1 %all_to_all.38 = f32[8,128,256]{2,0,1:T(8,128)S(1)} all-to-all(f32[8,128,256]{2,0,1:T(8,128)S(1)} %copy.12), channel_id=1, replica_groups=mesh['shard'=8,'tensor'=4] {'tensor'}, dimensions={1} | all-to-all | bytes 2097152 | tf_op jit(solution)/shard_map/all_to_all | solution.py:44
  57.9 0.9 multiply_reduce_fusion
  58.8 6.7 %psum.7 = f32[]{:T(128)} all-reduce(f32[]{:T(128)} %multiply_reduce_fusion), channel_id=1, replica_groups=mesh['shard'=8,'tensor'=4] {'tensor'}, use_global_device_ids=true, to_apply=%region_1.0 | all-reduce | flops 1 | bytes 8 | tf_op jit(solution)/shard_map/psum | solution.py:49
  66.2 0.7 copy.13
  66.9 1.2 copy.16
  68.2 34.0 %all-gather.7.cloned.1.call-done = f32[1024,1024]{1,0:T(8,128)} async-done(((f32[256,1024]{1,0:T(8,128)}), f32[1024,1024]{1,0:T(8,128)}) %all-gather.7.cloned.1.call-update) | async-done | bytes 4194320 | tf_op jit(solution)/shard_map/all_gather | solution.py:52
  102.1 7.3 %fusion.4 = f32[256,1024]{1,0:T(8,128)} fusion(f32[256,1024]{1,0:T(8,128)} %bitcast.33, f32[1024,1024]{1,0:T(8,128)} %all-gather.7.cloned.1.call-done), kind=kOutput, calls=%fused_computation.14 | convolution fusion | flops 3221225472 | bytes 6291456 | tf_op jit(solution)/shard_map/ij,lj->il/dot_general | solution.py:30
  109.4 0.6 all-gather.11.cloned.1.call-start
  110.0 34.1 %all-gather.9.cloned.1.call-done = f32[1024,1024]{1,0:T(8,128)} async-done(((f32[256,1024]{1,0:T(8,128)}), f32[1024,1024]{1,0:T(8,128)}) %all-gather.9.cloned.1.call-update) | async-done | bytes 4194320 | tf_op jit(solution)/shard_map/all_gather | solution.py:54
  144.1 6.7 %fusion.3 = f32[256,1024]{1,0:T(8,128)S(1)} fusion(f32[256,1024]{1,0:T(8,128)} %fusion.4, f32[1024,1024]{1,0:T(8,128)} %all-gather.9.cloned.1.call-done), kind=kOutput, calls=%fused_computation.9 | convolution fusion | flops 3222011904 | bytes 6291456 | tf_op jit(solution)/shard_map/ij,jl->il/dot_general | solution.py:20
  150.8 4.7 %convolution_add_fusion.2 = f32[256,1024]{1,0:T(8,128)} fusion(f32[256,1024]{1,0:T(8,128)S(1)} %fusion.3, f32[1024,1024]{1,0:T(8,128)S(1)} %copy-done, f32[256,1024]{1,0:T(8,128)S(1)} %bitcast.34), kind=kOutput, calls=%fused_computation.7 | convolution fusion | flops 3221749760 | bytes 7340032 | tf_op jit(solution)/shard_map/ij,jl->il/dot_general | solution.py:20
  155.5 34.6 %all-gather.11.cloned.1.call-done = f32[1024,1024]{1,0:T(8,128)} async-done(((f32[256,1024]{1,0:T(8,128)}), f32[1024,1024]{1,0:T(8,128)}) %all-gather.11.cloned.1.call-update) | async-done | bytes 4194320 | tf_op jit(solution)/shard_map/all_gather | solution.py:52
  190.1 7.3 %fusion.5 = f32[256,1024]{1,0:T(8,128)} fusion(f32[256,1024]{1,0:T(8,128)} %convolution_add_fusion.2, f32[1024,1024]{1,0:T(8,128)} %all-gather.11.cloned.1.call-done), kind=kOutput, calls=%fused_computation.15 | convolution fusion | flops 3221225472 | bytes 6291456 | tf_op jit(solution)/shard_map/ij,lj->il/dot_general | solution.py:30
  197.6 34.4 %all-gather.13.cloned.1.call-done = f32[1024,1024]{1,0:T(8,128)} async-done(((f32[256,1024]{1,0:T(8,128)}), f32[1024,1024]{1,0:T(8,128)}) %all-gather.13.cloned.1.call-update) | async-done | bytes 4194320 | tf_op jit(solution)/shard_map/all_gather | solution.py:54
  232.1 6.7 %fusion.2 = f32[256,1024]{1,0:T(8,128)S(1)} fusion(f32[256,1024]{1,0:T(8,128)} %fusion.5, f32[1024,1024]{1,0:T(8,128)} %all-gather.13.cloned.1.call-done), kind=kOutput, calls=%fused_computation.6 | convolution fusion | flops 3222011904 | bytes 6291456 | tf_op jit(solution)/shard_map/ij,jl->il/dot_general | solution.py:20
  238.8 4.7 %convolution_add_fusion.1 = f32[256,1024]{1,0:T(8,128)} fusion(f32[256,1024]{1,0:T(8,128)S(1)} %fusion.2, f32[1024,1024]{1,0:T(8,128)S(1)} %copy-done.1, f32[256,1024]{1,0:T(8,128)S(1)} %copy-done.3), kind=kOutput, calls=%fused_computation.4 | convolution fusion | flops 3221749760 | bytes 7340032 | tf_op jit(solution)/shard_map/ij,jl->il/dot_general | solution.py:20
  243.8 34.4 %all-gather.15.cloned.1.call-done = f32[1024,1024]{1,0:T(8,128)} async-done(((f32[256,1024]{1,0:T(8,128)}), f32[1024,1024]{1,0:T(8,128)}) %all-gather.15.cloned.1.call-update) | async-done | bytes 4194320 | tf_op jit(solution)/shard_map/all_gather | solution.py:52
  278.1 7.3 %fusion.6 = f32[256,1024]{1,0:T(8,128)} fusion(f32[256,1024]{1,0:T(8,128)} %convolution_add_fusion.1, f32[1024,1024]{1,0:T(8,128)} %all-gather.15.cloned.1.call-done), kind=kOutput, calls=%fused_computation.16 | convolution fusion | flops 3221225472 | bytes 6291456 | tf_op jit(solution)/shard_map/ij,lj->il/dot_general | solution.py:30
  285.4 34.6 %all-gather.17.cloned.1.call-done = f32[1024,1024]{1,0:T(8,128)} async-done(((f32[256,1024]{1,0:T(8,128)}), f32[1024,1024]{1,0:T(8,128)}) %all-gather.17.cloned.1.call-update) | async-done | bytes 4194320 | tf_op jit(solution)/shard_map/all_gather | solution.py:54
  320.1 6.7 %fusion.1 = f32[256,1024]{1,0:T(8,128)S(1)} fusion(f32[256,1024]{1,0:T(8,128)} %fusion.6, f32[1024,1024]{1,0:T(8,128)} %all-gather.17.cloned.1.call-done), kind=kOutput, calls=%fused_computation.3 | convolution fusion | flops 3222011904 | bytes 6291456 | tf_op jit(solution)/shard_map/ij,jl->il/dot_general | solution.py:20
  326.8 3.8 fusion
  330.6 29.3 %all_to_all.39 = f32[8,32,1024]{2,1,0:T(8,128)S(1)} all-to-all(f32[8,32,1024]{2,1,0:T(8,128)S(1)} %bitcast.35), channel_id=1, replica_groups=mesh['shard'=8,'tensor'=4] {'shard'}, dimensions={0} | all-to-all | bytes 2097152 | tf_op jit(solution)/shard_map/all_to_all | solution.py:60
  359.9 2.7 copy.14
  362.6 3.9 reshape.15
  366.5 18.1 %all_to_all.40 = f32[4,1,65536]{2,1,0:T(1,128)S(1)} all-to-all(f32[4,1,65536]{2,1,0:T(1,128)S(1)} %reshape.15), channel_id=1, replica_groups=mesh['shard'=8,'tensor'=4] {'tensor'}, dimensions={0} | all-to-all | bytes 2097152 | tf_op jit(solution)/shard_map/all_to_all | solution.py:59
  384.6 0.5 broadcast.34
  385.1 3.7 reduce.3
  388.8 3.4 reshape.16
  392.2 3.6 copy.15
  (24 shorter events, 0.8 us)
Async XLA Ops:
  7.2 95.0 %all-gather.7.cloned.1.call-start = ((), (), s32[]{:S(2)}) async-start(), calls=%async_computation.4 | async-start | bytes 5242880 | tf_op jit(solution)/shard_map/all_gather | solution.py:52
  68.1 75.9 %all-gather.9.cloned.1.call-start = ((), (), s32[]{:S(2)}) async-start(), calls=%async_computation.5 | async-start | bytes 5242880 | tf_op jit(solution)/shard_map/all_gather | solution.py:54
  109.4 41.4 %copy-start.5 = (f32[32,8,4,256]{3,1,2,0:T(8,128)S(1)}, f32[32,8,4,256]{3,1,2,0:T(8,128)}, u32[]{:S(2)}) copy-start(f32[32,8,4,256]{3,1,2,0:T(8,128)} %copy.16) | copy-start | bytes 3145732
  109.4 80.7 %all-gather.11.cloned.1.call-start = ((), (), s32[]{:S(2)}) async-start(), calls=%async_computation.6 | async-start | bytes 5242880 | tf_op jit(solution)/shard_map/all_gather | solution.py:52
  144.1 6.7 %copy-start = (f32[1024,1024]{1,0:T(8,128)S(1)}, f32[1024,1024]{1,0:T(8,128)}, u32[]{:S(2)}) copy-start(f32[1024,1024]{1,0:T(8,128)} %all-gather.7.cloned.1.call-done) | copy-start | bytes 12582916
  155.5 76.6 %all-gather.13.cloned.1.call-start = ((), (), s32[]{:S(2)}) async-start(), calls=%async_computation.7 | async-start | bytes 5242880 | tf_op jit(solution)/shard_map/all_gather | solution.py:54
  197.4 41.4 %copy-start.3 = (f32[256,1024]{1,0:T(8,128)S(1)}, f32[256,1024]{1,0:T(8,128)}, u32[]{:S(2)}) copy-start(f32[256,1024]{1,0:T(8,128)} %convolution_add_fusion.2) | copy-start | bytes 3145732
  197.4 80.7 %all-gather.15.cloned.1.call-start = ((), (), s32[]{:S(2)}) async-start(), calls=%async_computation.8 | async-start | bytes 5242880 | tf_op jit(solution)/shard_map/all_gather | solution.py:52
  232.1 6.7 %copy-start.1 = (f32[1024,1024]{1,0:T(8,128)S(1)}, f32[1024,1024]{1,0:T(8,128)}, u32[]{:S(2)}) copy-start(f32[1024,1024]{1,0:T(8,128)} %all-gather.11.cloned.1.call-done) | copy-start | bytes 12582916
  243.5 76.6 %all-gather.17.cloned.1.call-start = ((), (), s32[]{:S(2)}) async-start(), calls=%async_computation.9 | async-start | bytes 5242880 | tf_op jit(solution)/shard_map/all_gather | solution.py:54
  285.4 41.4 %copy-start.4 = (f32[256,1024]{1,0:T(8,128)S(1)}, f32[256,1024]{1,0:T(8,128)}, u32[]{:S(2)}) copy-start(f32[256,1024]{1,0:T(8,128)} %convolution_add_fusion.1) | copy-start | bytes 3145732
  320.1 6.7 %copy-start.2 = (f32[1024,1024]{1,0:T(8,128)S(1)}, f32[1024,1024]{1,0:T(8,128)}, u32[]{:S(2)}) copy-start(f32[1024,1024]{1,0:T(8,128)} %all-gather.15.cloned.1.call-done) | copy-start | bytes 12582916
Sparse Core Ops, SparseCore 0:
  68.2 33.8 all-gather.6
  109.5 34.4 all-gather.8
  155.6 34.4 all-gather.10
  197.5 34.4 all-gather.12
  243.6 34.4 all-gather.14
  285.6 34.4 all-gather.16
where the time goes:
time: 410 us; the launch traced here: 403 us
  waiting for transfers between devices  206 us (50%)
  blocking collectives  102 us (25%)
  matrix products  55 us (13%)
  local copies, waits for them, and re-layouts  16.6 us (4%)
  between operations  15.2 us (4%)
  other arithmetic  7.17 us (2%)
    all_gather x3, waiting for transfers between devices, per_device(): full_gram = lax.all_gather(gram_rows, 'tensor', axis=0, tiled=True)  103 us
    all_gather x3, waiting for transfers between devices, per_device(): full_rows = lax.all_gather(iterate, 'tensor', axis=0, tiled=True)  103 us
    dot_general x6, matrix products, product(): jnp.einsum('ij,jl->il', left, right, precision=lax.Precision.HIGHEST, pre...  33.2 us
    all_to_all x1, blocking collectives, per_device(): lax.all_to_all(direction, 'shard', split_axis=0, concat_axis=0, tiled=True)  29.4 us
    all_to_all x1, blocking collectives, per_device(): lax.all_to_all(result, 'shard', split_axis=0, concat_axis=0, tiled=True)  29.3 us
    dot_general x3, matrix products, against(): jnp.einsum('ij,lj->il', left, right, precision=lax.Precision.HIGHEST, pre...  21.8 us
    all_to_all x1, blocking collectives, per_device(): lax.all_to_all(by_owner, 'tensor', split_axis=1, concat_axis=2, tiled=True)  18.1 us
    all_to_all x1, blocking collectives, per_device(): lax.all_to_all(lax.all_to_all(result, 'shard', split_axis=0, concat_axis=...  18.1 us
  transfers between devices with their start and end apart: 6, of which 6 were waited for; matrix products, arithmetic and copies ran while one was open for 0% of the time, Pallas kernels for 0%

commit v1 on v0

v1 whole, which is shorter than its diff:
```python
import functools
import math

import jax
import jax.numpy as jnp
from jax import lax
from jax.experimental import pallas as pl
from jax.experimental.pallas import tpu as pltpu
from jax.sharding import PartitionSpec as P

ITERS = 3
TILE = 256

first_coef = 3.4445
second_coef = -4.775
third_coef = 2.0315
decay_rate = 0.95


def halves(value):
    high = value.astype(jnp.bfloat16)
    low = (value - high.astype(jnp.float32)).astype(jnp.bfloat16)
    return high, low


def split_dot(left_pair, right_high, right_low, contract):
    rows, depth = left_pair.shape[1:]
    dims = (((1,), (contract,)), ((), ()))
    both = lax.dot_general(
        left_pair.reshape(2 * rows, depth), right_high, dims, preferred_element_type=jnp.float32
    )
    cross = lax.dot_general(left_pair[0], right_low, dims, preferred_element_type=jnp.float32)
    return both[:rows] + (both[rows:] + cross)


def upper_tile(step, count):
    row = jnp.int32(0)
    offset = jnp.int32(0)
    passed = 0
    for index in range(count - 1):
        passed += count - index
        beyond = (step >= passed).astype(jnp.int32)
        row += beyond
        offset += beyond * (count - index)
    return row, step - offset + row


def columns_of(index):
    return pl.ds(pl.multiple_of(index * TILE, TILE), TILE)


def put_symmetric(out, row, column, value):
    high, low = halves(value)
    out[row, 0, :, columns_of(column)] = high
    out[row, 1, :, columns_of(column)] = low
    high, low = halves(value.T)
    out[column, 0, :, columns_of(row)] = high
    out[column, 1, :, columns_of(row)] = low


def column_halves(matrix, column):
    count = matrix.shape[0]
    depth = count * TILE
    cols = columns_of(column)
    return (
        matrix[:, 0, :, cols].reshape(depth, TILE),
        matrix[:, 1, :, cols].reshape(depth, TILE),
    )


def symmetric_product(out, left, right, finish=None):
    count = left.shape[0]

    def body(step, carry):
        row, column = upper_tile(step, count)
        right_high, right_low = column_halves(right, column)
        value = split_dot(left[row], right_high, right_low, 0)
        if finish is not None:
            value = finish(row, column, value)
        put_symmetric(out, row, column, value)
        return carry

    lax.fori_loop(0, count * (count + 1) // 2, body, 0)


def gram_of(out, matrix):
    count = matrix.shape[0]

    def body(step, carry):
        row, column = upper_tile(step, count)
        value = split_dot(matrix[row], matrix[column, 0], matrix[column, 1], 1)
        put_symmetric(out, row, column, value)
        return carry

    lax.fori_loop(0, count * (count + 1) // 2, body, 0)


def polynomial_of(out, gram):
    def finish(row, column, square):
        cols = columns_of(column)
        tile = gram[row, 0, :, cols].astype(jnp.float32) + gram[row, 1, :, cols].astype(jnp.float32)
        value = second_coef * tile + third_coef * square
        rows_at = lax.broadcasted_iota(jnp.int32, (TILE, TILE), 0) + row * TILE
        cols_at = lax.broadcasted_iota(jnp.int32, (TILE, TILE), 1) + column * TILE
        return value + jnp.where(rows_at == cols_at, first_coef, 0.0)

    symmetric_product(out, gram, gram, finish)


def orthogonalize(own, result, whole, gram, poly, mixed, mine, scale):
    count = whole.shape[0]
    gram_of(gram, whole)
    for index in range(count):
        rows = slice(index * TILE, (index + 1) * TILE)
        high, low = halves(own[rows, :] * scale)
        mine[0, 0, rows, :] = high
        mine[0, 1, rows, :] = low
    for sweep in range(ITERS):
        polynomial_of(poly, gram)
        now, later = sweep % 2, (sweep + 1) % 2
        last = sweep == ITERS - 1

        def body(row, carry):
            value = split_dot(poly[row], mine[now, 0], mine[now, 1], 0)
            rows = pl.ds(pl.multiple_of(row * TILE, TILE), TILE)
            if last:
                result[rows, :] = 0.2 * math.sqrt(count * TILE) * value
            else:
                high, low = halves(value)
                mine[later, 0, rows, :] = high
                mine[later, 1, rows, :] = low
            return carry

        lax.fori_loop(0, count, body, 0)
        if not last:
            symmetric_product(mixed, poly, gram)
            symmetric_product(gram, mixed, poly)


def kernel(pieces, own, result, whole, gram, poly, mixed, mine):
    parts, height, width = pieces.shape
    count = height // TILE
    total = jnp.zeros((8, width), jnp.float32)
    for part in range(parts):
        for index in range(count):
            value = pieces[part, index * TILE : (index + 1) * TILE, :]
            total += jnp.sum((value * value).reshape(TILE // 8, 8, width), axis=0)
    scale = 1.0 / (jnp.sqrt(jnp.sum(total)) + 1e-07)
    for part in range(parts):
        cols = slice(part * width, (part + 1) * width)
        for index in range(count):
            high, low = halves(pieces[part, index * TILE : (index + 1) * TILE, :] * scale)
            whole[index, 0, :, cols] = high
            whole[index, 1, :, cols] = low
    orthogonalize(own, result, whole, gram, poly, mixed, mine, scale)


def per_device(gradient, momentum):
    widened = gradient.astype(jnp.float32)
    momentum_out = decay_rate * momentum + widened
    direction = widened + decay_rate * momentum_out
    blocks, rows, width = direction.shape
    by_owner = lax.all_to_all(direction, "shard", split_axis=0, concat_axis=0, tiled=True)
    own = by_owner.reshape(blocks * rows, width)
    pieces = lax.all_gather(own, "tensor", axis=0)
    height = own.shape[0]
    count = height // TILE
    square = pltpu.VMEM((count, 2, TILE, height), jnp.bfloat16)
    result = pl.pallas_call(
        kernel,
        out_shape=jax.ShapeDtypeStruct((height, width), jnp.float32),
        in_specs=[pl.BlockSpec(memory_space=pltpu.VMEM)] * 2,
        out_specs=pl.BlockSpec(memory_space=pltpu.VMEM),
        scratch_shapes=[
            pltpu.VMEM((count, 2, TILE, pieces.shape[0] * width), jnp.bfloat16),
            square,
            square,
            square,
            pltpu.VMEM((2, 2, height, width), jnp.bfloat16),
        ],
        compiler_params=pltpu.CompilerParams(vmem_limit_bytes=50 * 1024 * 1024),
    )(pieces, own)
    update = lax.all_to_all(
        result.reshape(blocks, rows, width), "shard", split_axis=0, concat_axis=0, tiled=True
    )
    return (momentum_out, update)


def solution(mesh):
    placed = P(None, "shard", "tensor")
    return jax.shard_map(
        per_device,
        mesh=mesh,
        in_specs=(placed, placed),
        out_specs=(placed, placed),
        check_vma=False,
    )
```

time: 410 us -> 182 us (0.44)
  waiting for transfers between devices: 206 us -> 35.9 us
  Pallas kernels: 0 us -> 65 us
  matrix products: 55 us -> 0 us
  blocking collectives: 102 us -> 58.8 us
  local copies, waits for them, and re-layouts: 16.6 us -> 2.19 us
  other arithmetic: 7.17 us -> 2.54 us
    all_gather x6 -> x1, waiting for transfers between devices: 206 us -> 35.9 us  [per_device(): pieces = lax.all_gather(own, 'tensor', axis=0)]
    pallas_call x0 -> x1, Pallas kernels: none -> 65 us  [per_device(): pl.pallas_call(kernel, out_shape=jax.ShapeDtypeStruct((height, width), jn...]
    dot_general x9 -> x0, matrix products: 55 us -> none  [the longest x6 33.2 us: product(): jnp.einsum('ij,jl->il', left, right, precision=lax.Precision.HIGHEST, pre...]
    all_to_all x3 -> x1, blocking collectives: 65.6 us -> 29.3 us  [per_device(): lax.all_to_all(result.reshape(blocks, rows, width), 'shard', split_axis=0...]
    all_to_all x4 -> x0, local copies, waits for them, and re-layouts: 7.42 us -> none  [the longest x2 4.11 us: per_device(): lax.all_to_all(lax.all_to_all(result, 'shard', split_axis=0, concat_axis=...]
    psum x1 -> x0, blocking collectives: 6.66 us -> none  [per_device(): norm_total = lax.psum(jnp.sum(iterate * iterate), 'tensor')]
    unnamed x15 -> x3, local copies, waits for them, and re-layouts: 8.52 us -> 2.19 us
  transfers between devices with their start and end apart: 6 -> 1, of which waited for: 6 -> 1; matrix products, arithmetic and copies ran while one was open for 0% -> 0% of each run, Pallas kernels for 0% -> 0%
where the time goes in v1:
time: 182 us; the launch traced here: 179 us
  Pallas kernels  65 us (36%)
  blocking collectives  58.8 us (32%)
  waiting for transfers between devices  35.9 us (20%)
  between operations  14 us (8%)
  other arithmetic  2.54 us (1%)
  local copies, waits for them, and re-layouts  2.19 us (1%)
    pallas_call x1, Pallas kernels, per_device(): pl.pallas_call(kernel, out_shape=jax.ShapeDtypeStruct((height, width), jn...  65 us
    all_gather x1, waiting for transfers between devices, per_device(): pieces = lax.all_gather(own, 'tensor', axis=0)  35.9 us
    all_to_all x1, blocking collectives, per_device(): lax.all_to_all(direction, 'shard', split_axis=0, concat_axis=0, tiled=True)  29.5 us
    all_to_all x1, blocking collectives, per_device(): lax.all_to_all(result.reshape(blocks, rows, width), 'shard', split_axis=0...  29.3 us
  transfers between devices with their start and end apart: 1, of which 1 were waited for; matrix products, arithmetic and copies ran while one was open for 0% of the time, Pallas kernels for 0%

profile of v1, /device:TPU:9, one launch (start us, length us, event | category | flops | bytes accessed | tf_op | source)
XLA Modules:
  0.0 178.6 jit_solution(14396890277319341740)
XLA Ops:
  7.2 0.0 all-gather.2.cloned.1.call-start
  7.2 2.5 %convert_add_fusion = (f32[8,128,256]{2,1,0:T(8,128)S(1)}, f32[8,128,256]{2,1,0:T(8,128)}) fusion(bf16[8,128,256]{2,1,0:T(8,128)(2,1)} %param.2, f32[8,128,256]{2,1,0:T(8,128)} %param.3), kind=kLoop, calls=%fused_computation | loop fusion | flops 1310720 | bytes 3670016 | tf_op jit(solution)/shard_map/add | solution.py:161
  9.8 29.5 %all_to_all.10 = f32[8,128,256]{2,1,0:T(8,128)} all-to-all(f32[8,128,256]{2,1,0:T(8,128)S(1)} %get-tuple-element.2), channel_id=1, replica_groups=mesh['shard'=8,'tensor'=4] {'shard'}, dimensions={0} | all-to-all | bytes 2097152 | tf_op jit(solution)/shard_map/all_to_all | solution.py:163
  39.3 0.0 all-gather.2.cloned.1.call-update
  39.3 35.9 %all-gather.2.cloned.1.call-done.pieces = f32[4,1024,256]{2,1,0:T(8,128)} async-done(((f32[1,1024,256]{2,1,0:T(8,128)}), f32[4,1024,256]{2,1,0:T(8,128)}) %all-gather.2.cloned.1.call-update) | async-done | bytes 4194320 | tf_op jit(solution)/shard_map/all_gather | solution.py:165
  75.2 0.0 copy-start
  75.2 1.2 copy-done
  76.5 65.0 %shard_map.41 = f32[1024,256]{1,0:T(8,128)S(1)} custom-call(f32[4,1024,256]{2,1,0:T(8,128)} %all-gather.2.cloned.1.call-done.pieces, f32[1024,256]{1,0:T(8,128)S(1)} %bitcast.4), custom_call_target="tpu_custom_call" | custom-call | tf_op jit(solution)/shard_map/pallas_call | solution.py:169
  141.5 29.3 %all_to_all.11 = f32[8,128,256]{2,1,0:T(8,128)S(1)} all-to-all(f32[8,128,256]{2,1,0:T(8,128)S(1)} %bitcast.5), channel_id=1, replica_groups=mesh['shard'=8,'tensor'=4] {'shard'}, dimensions={0} | all-to-all | bytes 2097152 | tf_op jit(solution)/shard_map/all_to_all | solution.py:183
  170.8 1.0 copy.5
Async XLA Ops:
  7.2 68.1 %all-gather.2.cloned.1.call-start = ((), (), s32[]{:S(2)}) async-start(), calls=%async_computation.2 | async-start | bytes 5242880 | tf_op jit(solution)/shard_map/all_gather | solution.py:165
  75.2 1.2 copy-start
Sparse Core Ops, SparseCore 0:
  39.4 35.7 all-gather.1

commit v2 on v1

--- a/solution.py
+++ b/solution.py
@@ -83,12 +83,12 @@
     lax.fori_loop(0, count * (count + 1) // 2, body, 0)
 
 
-def gram_of(out, matrix):
+def gram_of(out, matrix, factor):
     count = matrix.shape[0]
 
     def body(step, carry):
         row, column = upper_tile(step, count)
-        value = split_dot(matrix[row], matrix[column, 0], matrix[column, 1], 1)
+        value = split_dot(matrix[row], matrix[column, 0], matrix[column, 1], 1) * factor
         put_symmetric(out, row, column, value)
         return carry
 
@@ -107,89 +107,190 @@
     symmetric_product(out, gram, gram, finish)
 
 
-def orthogonalize(own, result, whole, gram, poly, mixed, mine, scale):
+def orthogonalize(result, whole, gram, poly, mixed, mine, scale, order, send):
     count = whole.shape[0]
-    gram_of(gram, whole)
-    for index in range(count):
-        rows = slice(index * TILE, (index + 1) * TILE)
-        high, low = halves(own[rows, :] * scale)
-        mine[0, 0, rows, :] = high
-        mine[0, 1, rows, :] = low
+    gram_of(gram, whole, scale * scale)
     for sweep in range(ITERS):
         polynomial_of(poly, gram)
         now, later = sweep % 2, (sweep + 1) % 2
-        last = sweep == ITERS - 1
-
-        def body(row, carry):
-            value = split_dot(poly[row], mine[now, 0], mine[now, 1], 0)
-            rows = pl.ds(pl.multiple_of(row * TILE, TILE), TILE)
-            if last:
-                result[rows, :] = 0.2 * math.sqrt(count * TILE) * value
-            else:
+        if sweep < ITERS - 1:
+
+            def body(row, carry):
+                value = split_dot(poly[row], mine[now, 0], mine[now, 1], 0)
                 high, low = halves(value)
+                rows = pl.ds(pl.multiple_of(row * TILE, TILE), TILE)
                 mine[later, 0, rows, :] = high
                 mine[later, 1, rows, :] = low
-            return carry
-
-        lax.fori_loop(0, count, body, 0)
-        if not last:
+                return carry
+
+            lax.fori_loop(0, count, body, 0)
             symmetric_product(mixed, poly, gram)
             symmetric_product(gram, mixed, poly)
-
-
-def kernel(pieces, own, result, whole, gram, poly, mixed, mine):
-    parts, height, width = pieces.shape
+        else:
+            for row in order:
+                value = split_dot(poly[row], mine[now, 0], mine[now, 1], 0)
+                rows = pl.ds(pl.multiple_of(row * TILE, TILE), TILE)
+                result[rows, :] = (0.2 * math.sqrt(count * TILE) * scale) * value
+                send(row)
+
+
+def step_order(count):
+    half = count // 2
+    return [0] + [d for k in range(half) for d in (half + k, k) if d > 0]
+
+
+def kernel(shards, direction, update, pieces, result, whole, gram, poly, mixed, mine, sends, arrivals):
+    rows, width = direction.shape[1:]
+    height = shards * rows
     count = height // TILE
+    each = TILE // rows
+    me = lax.axis_index("shard")
+    lane = lax.axis_index("tensor")
+    order = step_order(shards)
+
+    def remote(src, dst, kind, step, target):
+        return pltpu.make_async_remote_copy(
+            src_ref=src,
+            dst_ref=dst,
+            send_sem=sends.at[kind, step],
+            recv_sem=arrivals.at[kind, step],
+            device_id=target,
+            device_id_type=pl.DeviceIdType.MESH,
+        )
+
+    barrier = pltpu.get_barrier_semaphore()
+    for step in range(1, shards):
+        pl.semaphore_signal(
+            barrier, inc=1, device_id=(me ^ step, lane), device_id_type=pl.DeviceIdType.MESH
+        )
+    for flip in (1, 2):
+        pl.semaphore_signal(
+            barrier, inc=1, device_id=(me, lane ^ flip), device_id_type=pl.DeviceIdType.MESH
+        )
+    pl.semaphore_wait(barrier, shards + 1)
+
+    def place(step):
+        return pl.ds(pl.multiple_of((me ^ step) * rows, rows), rows)
+
+    def mine_rows(step):
+        return pl.ds(pl.multiple_of(me * rows, rows), rows)
+
+    scatter = {}
+    for step in order[1:]:
+        scatter[step] = remote(
+            direction.at[me ^ step], pieces.at[lane, mine_rows(step)], 0, step, (me ^ step, lane)
+        )
+        scatter[step].start()
+
     total = jnp.zeros((8, width), jnp.float32)
-    for part in range(parts):
-        for index in range(count):
-            value = pieces[part, index * TILE : (index + 1) * TILE, :]
-            total += jnp.sum((value * value).reshape(TILE // 8, 8, width), axis=0)
+
+    def take(value, step, part, total):
+        source = me ^ step
+        block = lax.div(source, each)
+        inner = pl.ds(pl.multiple_of(lax.rem(source, each) * rows, rows), rows)
+        cols = pl.ds(pl.multiple_of(part * width, width), width)
+        high, low = halves(value)
+        whole[block, 0, inner, cols] = high
+        whole[block, 1, inner, cols] = low
+        return total + jnp.sum((value * value).reshape(rows // 8, 8, width), axis=0), high, low
+
+    forward = {}
+    for index in range(shards + 2):
+        if index < shards:
+            step = order[index]
+            if step == 0:
+                src = direction.at[me]
+            else:
+                scatter[step].wait_recv()
+                src = pieces.at[lane, place(step)]
+            for kind in (2, 1):
+                forward[kind, step] = remote(
+                    src, pieces.at[lane, place(step)], kind, step, (me, lane ^ kind)
+                )
+                forward[kind, step].start()
+            total, high, low = take(src[...], step, lane, total)
+            mine[0, 0, place(step), :] = high
+            mine[0, 1, place(step), :] = low
+        if 1 <= index <= shards:
+            step = order[index - 1]
+            forward[2, step].wait_recv()
+            src = pieces.at[lane ^ 2, place(step)]
+            forward[3, step] = remote(src, src, 3, step, (me, lane ^ 1))
+            forward[3, step].start()
+            total, _, _ = take(src[...], step, lane ^ 2, total)
+            forward[1, step].wait_recv()
+            total, _, _ = take(pieces[lane ^ 1, place(step), :], step, lane ^ 1, total)
+        if index >= 2:
+            step = order[index - 2]
+            forward[3, step].wait_recv()
+            total, _, _ = take(pieces[lane ^ 3, place(step), :], step, lane ^ 3, total)
     scale = 1.0 / (jnp.sqrt(jnp.sum(total)) + 1e-07)
-    for part in range(parts):
-        cols = slice(part * width, (part + 1) * width)
-        for index in range(count):
-            high, low = halves(pieces[part, index * TILE : (index + 1) * TILE, :] * scale)
-            whole[index, 0, :, cols] = high
-            whole[index, 1, :, cols] = low
-    orthogonalize(own, result, whole, gram, poly, mixed, mine, scale)
-
-
-def per_device(gradient, momentum):
+
+    home = lax.div(me, each)
+    back = {}
+
+    def back_copy(step):
+        return remote(result.at[place(step)], update.at[me], 4, step, (me ^ step, lane))
+
+    flips = list(range(count // 2, count)) + list(range(count // 2))[::-1]
+    sent = iter(flips)
+
+    def send(row):
+        flip = next(sent)
+        for inner in range(each):
+            step = flip * each + inner
+            if step == 0:
+                update[me] = result[mine_rows(step), :]
+            else:
+                back[step] = back_copy(step)
+                back[step].start()
+
+    orthogonalize(
+        result, whole, gram, poly, mixed, mine, scale, [home ^ flip for flip in flips], send
+    )
+    for step in order[1:]:
+        back[step].wait()
+    for copy in list(scatter.values()) + list(forward.values()):
+        copy.wait_send()
+
+
+def per_device(shards, gradient, momentum):
     widened = gradient.astype(jnp.float32)
     momentum_out = decay_rate * momentum + widened
     direction = widened + decay_rate * momentum_out
     blocks, rows, width = direction.shape
-    by_owner = lax.all_to_all(direction, "shard", split_axis=0, concat_axis=0, tiled=True)
-    own = by_owner.reshape(blocks * rows, width)
-    pieces = lax.all_gather(own, "tensor", axis=0)
-    height = own.shape[0]
+    height = blocks * rows
     count = height // TILE
+    parts = 4
     square = pltpu.VMEM((count, 2, TILE, height), jnp.bfloat16)
-    result = pl.pallas_call(
-        kernel,
-        out_shape=jax.ShapeDtypeStruct((height, width), jnp.float32),
-        in_specs=[pl.BlockSpec(memory_space=pltpu.VMEM)] * 2,
+    update = pl.pallas_call(
+        functools.partial(kernel, shards),
+        out_shape=jax.ShapeDtypeStruct((blocks, rows, width), jnp.float32),
+        in_specs=[pl.BlockSpec(memory_space=pltpu.VMEM)],
         out_specs=pl.BlockSpec(memory_space=pltpu.VMEM),
         scratch_shapes=[
-            pltpu.VMEM((count, 2, TILE, pieces.shape[0] * width), jnp.bfloat16),
+            pltpu.VMEM((parts, height, width), jnp.float32),
+            pltpu.VMEM((height, width), jnp.float32),
+            pltpu.VMEM((count, 2, TILE, parts * width), jnp.bfloat16),
             square,
             square,
             square,
             pltpu.VMEM((2, 2, height, width), jnp.bfloat16),
+            pltpu.SemaphoreType.DMA((5, shards)),
+            pltpu.SemaphoreType.DMA((5, shards)),
         ],
-        compiler_params=pltpu.CompilerParams(vmem_limit_bytes=50 * 1024 * 1024),
-    )(pieces, own)
-    update = lax.all_to_all(
-        result.reshape(blocks, rows, width), "shard", split_axis=0, concat_axis=0, tiled=True
-    )
+        compiler_params=pltpu.CompilerParams(
+            collective_id=0, has_side_effects=True, vmem_limit_bytes=50 * 1024 * 1024
+        ),
+    )(direction)
     return (momentum_out, update)
 
 
 def solution(mesh):
     placed = P(None, "shard", "tensor")
+    assert mesh.shape["tensor"] == 4
     return jax.shard_map(
-        per_device,
+        functools.partial(per_device, mesh.shape["shard"]),
         mesh=mesh,
         in_specs=(placed, placed),
         out_specs=(placed, placed),

time: 182 us -> 129 us (0.71); the launches traced: 179 us -> 129 us
  Pallas kernels: 65 us -> 125 us
  blocking collectives: 58.8 us -> 0 us
  waiting for transfers between devices: 35.9 us -> 0 us
  between operations: 14 us -> 0.64 us
    pallas_call x1, Pallas kernels: 65 us -> 125 us  [per_device(): pl.pallas_call(functools.partial(kernel, shards), out_shape=jax.ShapeDtyp...]
    all_to_all x2 -> x0, blocking collectives: 58.8 us -> none  [the longest x1 29.5 us: per_device(): lax.all_to_all(direction, 'shard', split_axis=0, concat_axis=0, tiled=True)]
    all_gather x1 -> x0, waiting for transfers between devices: 35.9 us -> none  [per_device(): pieces = lax.all_gather(own, 'tensor', axis=0)]
  transfers between devices with their start and end apart: 1 -> 0, of which waited for: 1 -> 0; matrix products, arithmetic and copies ran while one was open for 0% -> 0% of each run, Pallas kernels for 0% -> 0%
where the time goes in v2:
time: 129 us
  Pallas kernels  125 us (97%)
  other arithmetic  2.59 us (2%)
    pallas_call x1, Pallas kernels, per_device(): pl.pallas_call(functools.partial(kernel, shards), out_shape=jax.ShapeDtyp...  125 us
    add x1, other arithmetic, per_device(): direction = widened + decay_rate * momentum_out  2.59 us

profile of v2, /device:TPU:9, one launch (start us, length us, event | category | flops | bytes accessed | tf_op | source)
XLA Modules:
  0.0 129.2 jit_solution(17717571777592057372)
XLA Ops:
  0.6 2.6 %convert_add_fusion = (f32[8,128,256]{2,1,0:T(8,128)S(1)}, f32[8,128,256]{2,1,0:T(8,128)}) fusion(bf16[8,128,256]{2,1,0:T(8,128)(2,1)} %param.2, f32[8,128,256]{2,1,0:T(8,128)} %param.3), kind=kLoop, calls=%fused_computation | loop fusion | flops 1310720 | bytes 3670016 | tf_op jit(solution)/shard_map/add | solution.py:260
  3.2 125.0 %shard_map.41 = f32[8,128,256]{2,1,0:T(8,128)S(1)} custom-call(f32[8,128,256]{2,1,0:T(8,128)S(1)} %get-tuple-element.2.direction), custom_call_target="tpu_custom_call" | custom-call | tf_op jit(solution)/shard_map/pallas_call | solution.py:266
  128.2 1.0 copy.5

commit v3 on v2

--- a/solution.py
+++ b/solution.py
@@ -33,26 +33,20 @@
     return both[:rows] + (both[rows:] + cross)
 
 
-def upper_tile(step, count):
-    row = jnp.int32(0)
-    offset = jnp.int32(0)
-    passed = 0
-    for index in range(count - 1):
-        passed += count - index
-        beyond = (step >= passed).astype(jnp.int32)
-        row += beyond
-        offset += beyond * (count - index)
-    return row, step - offset + row
+def upper_tiles(count):
+    return [(row, column) for column in range(count) for row in range(column + 1)]
 
 
 def columns_of(index):
-    return pl.ds(pl.multiple_of(index * TILE, TILE), TILE)
+    return pl.ds(index * TILE, TILE)
 
 
 def put_symmetric(out, row, column, value):
     high, low = halves(value)
     out[row, 0, :, columns_of(column)] = high
     out[row, 1, :, columns_of(column)] = low
+    if row == column:
+        return
     high, low = halves(value.T)
     out[column, 0, :, columns_of(row)] = high
     out[column, 1, :, columns_of(row)] = low
@@ -71,28 +65,20 @@
 def symmetric_product(out, left, right, finish=None):
     count = left.shape[0]
 
-    def body(step, carry):
-        row, column = upper_tile(step, count)
+    for row, column in upper_tiles(count):
         right_high, right_low = column_halves(right, column)
         value = split_dot(left[row], right_high, right_low, 0)
         if finish is not None:
             value = finish(row, column, value)
         put_symmetric(out, row, column, value)
-        return carry
-
-    lax.fori_loop(0, count * (count + 1) // 2, body, 0)
 
 
 def gram_of(out, matrix, factor):
     count = matrix.shape[0]
 
-    def body(step, carry):
-        row, column = upper_tile(step, count)
+    for row, column in upper_tiles(count):
         value = split_dot(matrix[row], matrix[column, 0], matrix[column, 1], 1) * factor
         put_symmetric(out, row, column, value)
-        return carry
-
-    lax.fori_loop(0, count * (count + 1) // 2, body, 0)
 
 
 def polynomial_of(out, gram):
@@ -100,8 +86,10 @@
         cols = columns_of(column)
         tile = gram[row, 0, :, cols].astype(jnp.float32) + gram[row, 1, :, cols].astype(jnp.float32)
         value = second_coef * tile + third_coef * square
-        rows_at = lax.broadcasted_iota(jnp.int32, (TILE, TILE), 0) + row * TILE
-        cols_at = lax.broadcasted_iota(jnp.int32, (TILE, TILE), 1) + column * TILE
+        if row != column:
+            return value
+        rows_at = lax.broadcasted_iota(jnp.int32, (TILE, TILE), 0)
+        cols_at = lax.broadcasted_iota(jnp.int32, (TILE, TILE), 1)
         return value + jnp.where(rows_at == cols_at, first_coef, 0.0)
 
     symmetric_product(out, gram, gram, finish)
@@ -114,16 +102,11 @@
         polynomial_of(poly, gram)
         now, later = sweep % 2, (sweep + 1) % 2
         if sweep < ITERS - 1:
-
-            def body(row, carry):
+            for row in range(count):
                 value = split_dot(poly[row], mine[now, 0], mine[now, 1], 0)
                 high, low = halves(value)
-                rows = pl.ds(pl.multiple_of(row * TILE, TILE), TILE)
-                mine[later, 0, rows, :] = high
-                mine[later, 1, rows, :] = low
-                return carry
-
-            lax.fori_loop(0, count, body, 0)
+                mine[later, 0, columns_of(row), :] = high
+                mine[later, 1, columns_of(row), :] = low
             symmetric_product(mixed, poly, gram)
             symmetric_product(gram, mixed, poly)
         else:

time: 129 us -> 107 us (0.83)
  Pallas kernels: 125 us -> 103 us
    pallas_call x1, Pallas kernels: 125 us -> 103 us  [per_device(): pl.pallas_call(functools.partial(kernel, shards), out_shape=jax.ShapeDtyp...]
where the time goes in v3:
time: 107 us
  Pallas kernels  103 us (96%)
  other arithmetic  2.59 us (2%)
    pallas_call x1, Pallas kernels, per_device(): pl.pallas_call(functools.partial(kernel, shards), out_shape=jax.ShapeDtyp...  103 us
    add x1, other arithmetic, per_device(): direction = widened + decay_rate * momentum_out  2.59 us

profile of v3, /device:TPU:9, one launch (start us, length us, event | category | flops | bytes accessed | tf_op | source)
XLA Modules:
  0.0 107.1 jit_solution(11945998717077642960)
XLA Ops:
  0.6 2.6 %convert_add_fusion = (f32[8,128,256]{2,1,0:T(8,128)S(1)}, f32[8,128,256]{2,1,0:T(8,128)}) fusion(bf16[8,128,256]{2,1,0:T(8,128)(2,1)} %param.2, f32[8,128,256]{2,1,0:T(8,128)} %param.3), kind=kLoop, calls=%fused_computation | loop fusion | flops 1310720 | bytes 3670016 | tf_op jit(solution)/shard_map/add | solution.py:243
  3.2 102.9 %shard_map.41 = f32[8,128,256]{2,1,0:T(8,128)S(1)} custom-call(f32[8,128,256]{2,1,0:T(8,128)S(1)} %get-tuple-element.2.direction), custom_call_target="tpu_custom_call" | custom-call | tf_op jit(solution)/shard_map/pallas_call | solution.py:249
  106.1 1.0 copy.5

commit v4 on v3

--- a/solution.py
+++ b/solution.py
@@ -73,12 +73,8 @@
         put_symmetric(out, row, column, value)
 
 
-def gram_of(out, matrix, factor):
-    count = matrix.shape[0]
-
-    for row, column in upper_tiles(count):
-        value = split_dot(matrix[row], matrix[column, 0], matrix[column, 1], 1) * factor
-        put_symmetric(out, row, column, value)
+def gram_tile(matrix, row, column):
+    return split_dot(matrix[row], matrix[column, 0], matrix[column, 1], 1)
 
 
 def polynomial_of(out, gram):
@@ -95,41 +91,51 @@
     symmetric_product(out, gram, gram, finish)
 
 
-def orthogonalize(result, whole, gram, poly, mixed, mine, scale, order, send):
-    count = whole.shape[0]
-    gram_of(gram, whole, scale * scale)
-    for sweep in range(ITERS):
+def joined(mine, slot, row):
+    rows = columns_of(row)
+    return mine[slot, 0, rows, :].astype(jnp.float32) + mine[slot, 1, rows, :].astype(jnp.float32)
+
+
+def put_rows(mine, slot, row, value):
+    high, low = halves(value)
+    mine[slot, 0, columns_of(row), :] = high
+    mine[slot, 1, columns_of(row), :] = low
+
+
+def orthogonalize(result, gram, poly, mixed, mine, scale, order, send):
+    count = gram.shape[0]
+    for sweep in range(ITERS - 1):
         polynomial_of(poly, gram)
         now, later = sweep % 2, (sweep + 1) % 2
-        if sweep < ITERS - 1:
-            for row in range(count):
-                value = split_dot(poly[row], mine[now, 0], mine[now, 1], 0)
-                high, low = halves(value)
-                mine[later, 0, columns_of(row), :] = high
-                mine[later, 1, columns_of(row), :] = low
-            symmetric_product(mixed, poly, gram)
-            symmetric_product(gram, mixed, poly)
-        else:
-            for row in order:
-                value = split_dot(poly[row], mine[now, 0], mine[now, 1], 0)
-                rows = pl.ds(pl.multiple_of(row * TILE, TILE), TILE)
-                result[rows, :] = (0.2 * math.sqrt(count * TILE) * scale) * value
-                send(row)
-
-
-def step_order(count):
+        for row in range(count):
+            put_rows(mine, later, row, split_dot(poly[row], mine[now, 0], mine[now, 1], 0))
+        symmetric_product(mixed, poly, gram)
+        symmetric_product(gram, mixed, poly)
+    now, later = (ITERS - 1) % 2, ITERS % 2
+    for row in range(count):
+        value = split_dot(gram[row], mine[now, 0], mine[now, 1], 0)
+        put_rows(mine, later, row, second_coef * joined(mine, now, row) + third_coef * value)
+    for row in order:
+        value = split_dot(gram[row], mine[later, 0], mine[later, 1], 0)
+        value = first_coef * joined(mine, now, row) + value
+        result[columns_of(row), :] = (0.2 * math.sqrt(count * TILE) * scale) * value
+        send(row)
+
+
+def block_order(count):
     half = count // 2
-    return [0] + [d for k in range(half) for d in (half + k, k) if d > 0]
-
-
-def kernel(shards, direction, update, pieces, result, whole, gram, poly, mixed, mine, sends, arrivals):
+    return [block for k in range(half) for block in (k, half + k)]
+
+
+def kernel(shards, direction, update, pieces, result, whole, gram, poly, mixed, mine, tiles, sends, arrivals):
     rows, width = direction.shape[1:]
     height = shards * rows
     count = height // TILE
     each = TILE // rows
     me = lax.axis_index("shard")
     lane = lax.axis_index("tensor")
-    order = step_order(shards)
+    blocks = block_order(count)
+    order = [block * each + inner for block in blocks for inner in range(each)]
 
     def remote(src, dst, kind, step, target):
         return pltpu.make_async_remote_copy(
@@ -153,31 +159,28 @@
     pl.semaphore_wait(barrier, shards + 1)
 
     def place(step):
-        return pl.ds(pl.multiple_of((me ^ step) * rows, rows), rows)
-
-    def mine_rows(step):
-        return pl.ds(pl.multiple_of(me * rows, rows), rows)
+        return pl.ds(step * rows, rows)
 
     scatter = {}
     for step in order[1:]:
         scatter[step] = remote(
-            direction.at[me ^ step], pieces.at[lane, mine_rows(step)], 0, step, (me ^ step, lane)
+            direction.at[me ^ step], pieces.at[lane, place(step)], 0, step, (me ^ step, lane)
         )
         scatter[step].start()
 
     total = jnp.zeros((8, width), jnp.float32)
 
     def take(value, step, part, total):
-        source = me ^ step
-        block = lax.div(source, each)
-        inner = pl.ds(pl.multiple_of(lax.rem(source, each) * rows, rows), rows)
-        cols = pl.ds(pl.multiple_of(part * width, width), width)
+        block = step // each
+        inner = pl.ds(step % each * rows, rows)
+        cols = pl.ds(part * width, width)
         high, low = halves(value)
         whole[block, 0, inner, cols] = high
         whole[block, 1, inner, cols] = low
         return total + jnp.sum((value * value).reshape(rows // 8, 8, width), axis=0), high, low
 
     forward = {}
+    placed = []
     for index in range(shards + 2):
         if index < shards:
             step = order[index]
@@ -191,7 +194,7 @@
                     src, pieces.at[lane, place(step)], kind, step, (me, lane ^ kind)
                 )
                 forward[kind, step].start()
-            total, high, low = take(src[...], step, lane, total)
+            total, high, low = take(src[...], step, 0, total)
             mine[0, 0, place(step), :] = high
             mine[0, 1, place(step), :] = low
         if 1 <= index <= shards:
@@ -200,37 +203,43 @@
             src = pieces.at[lane ^ 2, place(step)]
             forward[3, step] = remote(src, src, 3, step, (me, lane ^ 1))
             forward[3, step].start()
-            total, _, _ = take(src[...], step, lane ^ 2, total)
+            total, _, _ = take(src[...], step, 2, total)
             forward[1, step].wait_recv()
-            total, _, _ = take(pieces[lane ^ 1, place(step), :], step, lane ^ 1, total)
+            total, _, _ = take(pieces[lane ^ 1, place(step), :], step, 1, total)
         if index >= 2:
             step = order[index - 2]
             forward[3, step].wait_recv()
-            total, _, _ = take(pieces[lane ^ 3, place(step), :], step, lane ^ 3, total)
+            total, _, _ = take(pieces[lane ^ 3, place(step), :], step, 3, total)
+            complete = (index - 1) // each
+            if (index - 1) % each == 0 and complete < count:
+                row = blocks[complete - 1]
+                for column in blocks[:complete]:
+                    tiles[len(placed)] = gram_tile(whole, row, column)
+                    placed.append((row, column))
     scale = 1.0 / (jnp.sqrt(jnp.sum(total)) + 1e-07)
 
-    home = lax.div(me, each)
+    for slot, (row, column) in enumerate(placed):
+        put_symmetric(gram, row, column, tiles[slot] * (scale * scale))
+    for column in blocks:
+        value = gram_tile(whole, blocks[-1], column) * (scale * scale)
+        put_symmetric(gram, blocks[-1], column, value)
+
     back = {}
 
     def back_copy(step):
         return remote(result.at[place(step)], update.at[me], 4, step, (me ^ step, lane))
 
-    flips = list(range(count // 2, count)) + list(range(count // 2))[::-1]
-    sent = iter(flips)
-
     def send(row):
-        flip = next(sent)
         for inner in range(each):
-            step = flip * each + inner
+            step = row * each + inner
             if step == 0:
-                update[me] = result[mine_rows(step), :]
+                update[me] = result[place(step), :]
             else:
                 back[step] = back_copy(step)
                 back[step].start()
 
-    orthogonalize(
-        result, whole, gram, poly, mixed, mine, scale, [home ^ flip for flip in flips], send
-    )
+    farthest = list(range(count // 2, count)) + list(range(count // 2))[::-1]
+    orthogonalize(result, gram, poly, mixed, mine, scale, farthest, send)
     for step in order[1:]:
         back[step].wait()
     for copy in list(scatter.values()) + list(forward.values()):
@@ -259,6 +268,7 @@
             square,
             square,
             pltpu.VMEM((2, 2, height, width), jnp.bfloat16),
+            pltpu.VMEM((count * (count - 1) // 2, TILE, TILE), jnp.float32),
             pltpu.SemaphoreType.DMA((5, shards)),
             pltpu.SemaphoreType.DMA((5, shards)),
         ],

time: 107 us -> 95.8 us (0.90)
  Pallas kernels: 103 us -> 91.2 us
    pallas_call x1, Pallas kernels: 103 us -> 91.2 us  [per_device(): pl.pallas_call(functools.partial(kernel, shards), out_shape=jax.ShapeDtyp...]
where the time goes in v4:
time: 95.8 us; the launch traced here: 95.4 us
  Pallas kernels  91.2 us (95%)
  other arithmetic  2.59 us (3%)
  local copies, waits for them, and re-layouts  0.97 us (1%)
    pallas_call x1, Pallas kernels, per_device(): pl.pallas_call(functools.partial(kernel, shards), out_shape=jax.ShapeDtyp...  91.2 us
    add x1, other arithmetic, per_device(): direction = widened + decay_rate * momentum_out  2.59 us

profile of v4, /device:TPU:9, one launch (start us, length us, event | category | flops | bytes accessed | tf_op | source)
XLA Modules:
  0.0 95.4 jit_solution(8763992073744834202)
XLA Ops:
  0.6 2.6 %convert_add_fusion = (f32[8,128,256]{2,1,0:T(8,128)S(1)}, f32[8,128,256]{2,1,0:T(8,128)}) fusion(bf16[8,128,256]{2,1,0:T(8,128)(2,1)} %param.2, f32[8,128,256]{2,1,0:T(8,128)} %param.3), kind=kLoop, calls=%fused_computation | loop fusion | flops 1310720 | bytes 3670016 | tf_op jit(solution)/shard_map/add | solution.py:252
  3.2 91.2 %shard_map.41 = f32[8,128,256]{2,1,0:T(8,128)S(1)} custom-call(f32[8,128,256]{2,1,0:T(8,128)S(1)} %get-tuple-element.2.direction), custom_call_target="tpu_custom_call" | custom-call | tf_op jit(solution)/shard_map/pallas_call | solution.py:258
  94.4 1.0 %copy.5 = f32[8,128,256]{2,1,0:T(8,128)} copy(f32[8,128,256]{2,1,0:T(8,128)S(1)} %shard_map.41) | data formatting | bytes 2097152

commit v5 on v4

--- a/solution.py
+++ b/solution.py
@@ -166,6 +166,9 @@
         scatter[step] = remote(
             direction.at[me ^ step], pieces.at[lane, place(step)], 0, step, (me ^ step, lane)
         )
+
+    follows = dict(zip(order[each : 2 * each], order[-each:]))
+    for step in order[1:-each]:
         scatter[step].start()
 
     total = jnp.zeros((8, width), jnp.float32)
@@ -187,6 +190,9 @@
             if step == 0:
                 src = direction.at[me]
             else:
+                if step in follows:
+                    scatter[step].wait_send()
+                    scatter[follows[step]].start()
                 scatter[step].wait_recv()
                 src = pieces.at[lane, place(step)]
             for kind in (2, 1):
@@ -242,7 +248,10 @@
     orthogonalize(result, gram, poly, mixed, mine, scale, farthest, send)
     for step in order[1:]:
         back[step].wait()
-    for copy in list(scatter.values()) + list(forward.values()):
+    for step in order[1:]:
+        if step not in follows:
+            scatter[step].wait_send()
+    for copy in forward.values():
         copy.wait_send()
 
 

time: 95.8 us -> 95.8 us (level)
  no operation moved by 1% of the time
where the time goes in v5:
time: 95.8 us; the launch traced here: 95.4 us
  Pallas kernels  91.2 us (95%)
  other arithmetic  2.59 us (3%)
  local copies, waits for them, and re-layouts  0.97 us (1%)
    pallas_call x1, Pallas kernels, per_device(): pl.pallas_call(functools.partial(kernel, shards), out_shape=jax.ShapeDtyp...  91.2 us
    add x1, other arithmetic, per_device(): direction = widened + decay_rate * momentum_out  2.59 us

profile of v5, /device:TPU:9, one launch (start us, length us, event | category | flops | bytes accessed | tf_op | source)
XLA Modules:
  0.0 95.4 jit_solution(12970802663348593256)
XLA Ops:
  0.6 2.6 %convert_add_fusion = (f32[8,128,256]{2,1,0:T(8,128)S(1)}, f32[8,128,256]{2,1,0:T(8,128)}) fusion(bf16[8,128,256]{2,1,0:T(8,128)(2,1)} %param.2, f32[8,128,256]{2,1,0:T(8,128)} %param.3), kind=kLoop, calls=%fused_computation | loop fusion | flops 1310720 | bytes 3670016 | tf_op jit(solution)/shard_map/add | solution.py:261
  3.2 91.2 %shard_map.41 = f32[8,128,256]{2,1,0:T(8,128)S(1)} custom-call(f32[8,128,256]{2,1,0:T(8,128)S(1)} %get-tuple-element.2.direction), custom_call_target="tpu_custom_call" | custom-call | tf_op jit(solution)/shard_map/pallas_call | solution.py:267
  94.4 1.0 %copy.5 = f32[8,128,256]{2,1,0:T(8,128)} copy(f32[8,128,256]{2,1,0:T(8,128)S(1)} %shard_map.41) | data formatting | bytes 2097152
